TPU v7x, 32 devices: a whole 2x2x4 slice. The times are simulated.
32 devices in a mesh: ctx: 8 (over z, y), tp: 4 (over x, core).
Axes of the slice: x: 2, y: 2, z: 4, core: 2. Of those that a mesh axis runs over, the one named last changes fastest.
Arguments:
- query_rows: bfloat16 [2048, 64, 128], P('ctx', 'tp'), may hold values from -8 to 8
- key_rows: bfloat16 [2048, 8, 128], P('ctx', 'tp'), may hold values from -8 to 8
- value_rows: bfloat16 [2048, 8, 128], P('ctx', 'tp'), may hold values from -6 to 6
- grad_rows: bfloat16 [2048, 64, 128], P('ctx', 'tp'), may hold values from -6 to 6
- doc_ids: int32 [2048], replicated, may hold values from 0 to 8, as said below
Outputs:
- attended: bfloat16 [2048, 64, 128], P('ctx', 'tp')
- query_grad: bfloat16 [2048, 64, 128], P('ctx', 'tp')
- key_grad: bfloat16 [2048, 8, 128], P('ctx', 'tp')
- value_grad: bfloat16 [2048, 8, 128], P('ctx', 'tp')
- top_logit: float32 [], replicated
Inputs may be any that keep to these rules, and one draw needn't show every extreme that they name: `doc_ids`: ids start at 0 and rise by one at each document boundary, except that the last document takes the number 4 * 2; every document holds 256 to 1024 tokens, save the last, which may be shorter; one holds exactly 1024.
All inputs are finite; a program needn't handle non-finite values.
Results may differ from a plain program's by a relative error of at most 0.018.
Values may be sent and summed in bfloat16 or wider, within the bound.
A program may use at most 128 MiB of HBM per device.

v0:
```python
import functools
import math

import jax
import jax.numpy as jnp
from jax import lax
from jax.experimental import pallas as pl
from jax.experimental.pallas import tpu as pltpu
from jax.sharding import PartitionSpec as P

REACH = 4
ROWS = 256
NEGATIVE = -1e30
F32 = jnp.float32
BF16 = jnp.bfloat16
NT = (((1,), (1,)), ((), ()))


def shift(block, distance):
    devices = range(lax.axis_size("ctx"))
    route = [(i, i + distance) for i in devices if i + distance in devices]
    return lax.ppermute(block, "ctx", route)


def chunk_step(
    c, peak, g, heads, tokens, q_ref, do_ref, lo_ref, k_ref, v_ref, kt_ref, vt_ref,
    o_ref, dq_ref, dk_ref, dv_ref, s_ref, dp_ref, w_ref, ds_ref,
):
    tiles = k_ref.shape[1] // tokens
    width = k_ref.shape[2]
    scale = 1.0 / math.sqrt(width)
    base2 = scale * math.log2(math.e)
    rows = pl.ds(pl.multiple_of(c * ROWS, ROWS), ROWS)
    q = q_ref[g, rows, :]
    do = do_ref[g, rows, :]
    low = lo_ref[:, rows]
    key_place = lax.broadcasted_iota(jnp.int32, (tokens, ROWS), 0)
    query_place = (lax.broadcasted_iota(jnp.int32, (1, ROWS), 1) + c * ROWS) // heads
    top = jnp.full((1, ROWS), NEGATIVE, F32)
    for j in range(tiles):
        keys = pl.ds(j * tokens, tokens)
        s = lax.dot_general(k_ref[g, keys, :], q, NT, preferred_element_type=F32)
        allowed = key_place >= low + j * tokens
        if j == 0:
            allowed = allowed & (key_place <= query_place)
        s = jnp.where(allowed, s, NEGATIVE)
        s_ref[keys, :] = s
        top = jnp.maximum(top, jnp.max(s, axis=0, keepdims=True))
    total = jnp.zeros((1, ROWS), F32)
    dot = jnp.zeros((1, ROWS), F32)
    for j in range(tiles):
        keys = pl.ds(j * tokens, tokens)
        p = jnp.exp2((s_ref[keys, :] - top) * base2)
        dp = lax.dot_general(v_ref[g, keys, :], do, NT, preferred_element_type=F32)
        s_ref[keys, :] = p
        dp_ref[keys, :] = dp
        total = total + jnp.sum(p, axis=0, keepdims=True)
        dot = dot + jnp.sum(p * dp, axis=0, keepdims=True)
    inverse = 1.0 / total
    dot = dot * inverse
    for j in range(tiles):
        keys = pl.ds(j * tokens, tokens)
        p = s_ref[keys, :] * inverse
        w_ref[keys, :] = p.astype(BF16)
        ds_ref[keys, :] = (p * (dp_ref[keys, :] - dot)).astype(BF16)
    w = w_ref[...]
    ds = ds_ref[...]
    o = jnp.dot(vt_ref[...], w, preferred_element_type=F32)
    dq = jnp.dot(kt_ref[...], ds, preferred_element_type=F32) * scale
    o_ref[g, rows, :] = o.T.astype(BF16)
    dq_ref[g, rows, :] = dq.T.astype(BF16)
    dv_ref[...] += jnp.dot(w, do, preferred_element_type=F32)
    dk_ref[...] += jnp.dot(ds, q, preferred_element_type=F32)
    return jnp.maximum(peak, top)


def kernel(
    heads, tokens, q_ref, do_ref, lo_ref, k_ref, v_ref,
    o_ref, dq_ref, dk_out, dv_out, top_ref,
    kt_ref, vt_ref, dk_ref, dv_ref, s_ref, dp_ref, w_ref, ds_ref,
):
    groups, rows, width = q_ref.shape
    scale = 1.0 / math.sqrt(width)
    peak = jnp.full((1, ROWS), NEGATIVE, F32)
    for g in range(groups):
        kt_ref[...] = k_ref[g].T
        vt_ref[...] = v_ref[g].T
        dk_ref[...] = jnp.zeros_like(dk_ref)
        dv_ref[...] = jnp.zeros_like(dv_ref)
        step = functools.partial(
            chunk_step, g=g, heads=heads, tokens=tokens, q_ref=q_ref, do_ref=do_ref,
            lo_ref=lo_ref, k_ref=k_ref, v_ref=v_ref, kt_ref=kt_ref, vt_ref=vt_ref,
            o_ref=o_ref, dq_ref=dq_ref, dk_ref=dk_ref, dv_ref=dv_ref, s_ref=s_ref,
            dp_ref=dp_ref, w_ref=w_ref, ds_ref=ds_ref,
        )
        peak = lax.fori_loop(0, rows // ROWS, step, peak)
        dk_out[g] = (dk_ref[...] * scale).astype(BF16)
        dv_out[g] = dv_ref[...].astype(BF16)
    top_ref[...] = jnp.broadcast_to(jnp.max(peak, axis=1, keepdims=True) * scale, top_ref.shape)


def shards(query_rows, key_rows, value_rows, grad_rows, doc_ids):
    tokens, head_count, width = query_rows.shape
    groups = key_rows.shape[1]
    heads = head_count // groups
    me = lax.axis_index("ctx")
    own_ids = lax.dynamic_slice_in_dim(doc_ids, me * tokens, tokens, 0)
    first = jnp.sum((doc_ids[None, :] < own_ids[:, None]).astype(jnp.int32), axis=1)
    low = jnp.repeat(first - me * tokens, heads)[None, :]

    def by_group(x):
        return x.reshape(tokens, groups, heads, width).transpose(1, 0, 2, 3).reshape(groups, tokens * heads, width)

    def by_token(x):
        return x.reshape(groups, tokens, heads, width).transpose(1, 0, 2, 3).reshape(tokens, head_count, width)

    own = jnp.stack([key_rows, value_rows]).transpose(0, 2, 1, 3)
    blocks = [own] + [shift(own, d) for d in range(1, REACH + 1)]
    both = jnp.concatenate(blocks, axis=2)
    keys = both.shape[2]
    vmem = pl.BlockSpec(memory_space=pltpu.VMEM)
    attended, query_grad, dk, dv, top = pl.pallas_call(
        functools.partial(kernel, heads, tokens),
        out_shape=(
            jax.ShapeDtypeStruct((groups, tokens * heads, width), BF16),
            jax.ShapeDtypeStruct((groups, tokens * heads, width), BF16),
            jax.ShapeDtypeStruct((groups, keys, width), BF16),
            jax.ShapeDtypeStruct((groups, keys, width), BF16),
            jax.ShapeDtypeStruct((8, 128), F32),
        ),
        in_specs=[vmem] * 5,
        out_specs=(vmem,) * 5,
        scratch_shapes=[
            pltpu.VMEM((width, keys), BF16),
            pltpu.VMEM((width, keys), BF16),
            pltpu.VMEM((keys, width), F32),
            pltpu.VMEM((keys, width), F32),
            pltpu.VMEM((keys, ROWS), F32),
            pltpu.VMEM((keys, ROWS), F32),
            pltpu.VMEM((keys, ROWS), BF16),
            pltpu.VMEM((keys, ROWS), BF16),
        ],
        compiler_params=pltpu.CompilerParams(vmem_limit_bytes=50 << 20),
    )(by_group(query_rows), by_group(grad_rows), low, both[0], both[1])
    parts = jnp.stack([dk, dv]).reshape(2, groups, REACH + 1, tokens, width)
    result = parts[:, :, 0].astype(F32)
    for d in range(1, REACH + 1):
        result = result + shift(parts[:, :, d], -d).astype(F32)
    result = result.transpose(0, 2, 1, 3).astype(BF16)
    top_logit = lax.pmax(top[0, 0], ("ctx", "tp"))
    return by_token(attended), by_token(query_grad), result[0], result[1], top_logit


def solution(mesh):
    part = P("ctx", "tp", None)
    return jax.shard_map(
        shards,
        mesh=mesh,
        in_specs=(part, part, part, part, P()),
        out_specs=(part, part, part, part, P()),
        check_vma=False,
    )
```

profile of v0, /device:TPU:8, one launch (start us, length us, event | category | flops | bytes accessed | tf_op | source)
XLA Modules:
  0.0 155.4 jit_solution(12733557364055683039)
XLA Ops:
  0.7 1.1 copy_bitcast_fusion.4
  1.8 4.5 %collective-permute-start.3 = (bf16[2,2,256,128]{3,2,1,0:T(8,128)(2,1)S(1)}, bf16[2,2,256,128]{3,2,1,0:T(8,128)(2,1)S(1)}, u32[]{:S(2)}, u32[]{:S(2)}) collective-permute-start(bf16[2,2,256,128]{3,2,1,0:T(8,128)(2,1)S(1)} %maximum_bitcast_fusion), channel_id=1, source_target_pairs={{0,16},{4,20},{8,24},{12,28},{1,17},{5,21},{9,25},{13,29},{2,18},{... | collective-permute-start | bytes 786440 | tf_op jit(solution)/shard_map/ppermute | solution.py:22
  6.4 1.3 collective-permute-start.2
  7.7 3.4 %collective-permute-start.1 = (bf16[2,2,256,128]{3,2,1,0:T(8,128)(2,1)S(1)}, bf16[2,2,256,128]{3,2,1,0:T(8,128)(2,1)}, u32[]{:S(2)}, u32[]{:S(2)}) collective-permute-start(bf16[2,2,256,128]{3,2,1,0:T(8,128)(2,1)S(1)} %maximum_bitcast_fusion), channel_id=1, source_target_pairs={{0,8},{4,12},{8,16},{12,20},{16,24},{20,28},{1,9},{5,13},{9,17},{1... | collective-permute-start | bytes 786440 | tf_op jit(solution)/shard_map/ppermute | solution.py:22
  11.1 2.6 %collective-permute-start = (bf16[2,2,256,128]{3,2,1,0:T(8,128)(2,1)S(1)}, bf16[2,2,256,128]{3,2,1,0:T(8,128)(2,1)}, u32[]{:S(2)}, u32[]{:S(2)}) collective-permute-start(bf16[2,2,256,128]{3,2,1,0:T(8,128)(2,1)S(1)} %maximum_bitcast_fusion), channel_id=1, source_target_pairs={{0,4},{4,8},{8,12},{12,16},{16,20},{20,24},{24,28},{1,5},{5,9},{9,... | collective-permute-start | bytes 786440 | tf_op jit(solution)/shard_map/ppermute | solution.py:22
  13.7 0.8 dynamic_slice.3
  14.4 1.0 convert_reduce_fusion
  15.5 1.7 %copy_bitcast_fusion.2 = (bf16[2,2048,128]{2,1,0:T(8,128)(2,1)}, bf16[2,2048,128]{2,1,0:T(8,128)(2,1)}) fusion(bf16[256,16,128]{2,1,0:T(8,128)(2,1)S(1)} %copy-done, bf16[256,16,128]{2,1,0:T(8,128)(2,1)S(1)} %copy-done.2), kind=kLoop, calls=%fused_computation.3 | loop fusion | bytes 4194304 | tf_op jit(solution)/shard_map/reshape | solution.py:112
  17.2 0.1 broadcast_in_dim.2
  17.3 0.1 broadcast_in_dim_reshape.3.lo_ref
  17.4 13.3 %collective-permute-done = bf16[2,2,256,128]{3,2,1,0:T(8,128)(2,1)} collective-permute-done((bf16[2,2,256,128]{3,2,1,0:T(8,128)(2,1)S(1)}, bf16[2,2,256,128]{3,2,1,0:T(8,128)(2,1)}, u32[]{:S(2)}, u32[]{:S(2)}) %collective-permute-start) | collective-permute-done | bytes 262176 | tf_op jit(solution)/shard_map/ppermute | solution.py:22
  30.8 1.0 constant_dynamic-update-slice_fusion.3
  31.8 1.0 constant_dynamic-update-slice_fusion.2
  32.9 0.1 slice_bitcast_fusion
  32.9 28.8 %shard_map.92 = (bf16[2,2048,128]{2,1,0:T(8,128)(2,1)S(1)}, bf16[2,2048,128]{2,1,0:T(8,128)(2,1)}, bf16[2,1280,128]{2,1,0:T(8,128)(2,1)S(1)}, bf16[2,1280,128]{2,1,0:T(8,128)(2,1)S(1)}, f32[8,128]{1,0:T(8,128)S(1)}) custom-call(bf16[2,2048,128]{2,1,0:T(8,128)(2,1)} %get-tuple-element.26.q_ref, bf16[2,2048,128]{2,1,0:T(8,128)(2,1)} %get-tuple-element.25.do_ref, ...), custom_call_target="tpu_custom_call" | custom-call | tf_op jit(solution)/shard_map/pallas_call | solution.py:122
  61.7 0.5 slice.39
  62.2 49.1 %pmax.7 = f32[]{:T(128)} all-reduce(f32[]{:T(128)} %bitcast.27), channel_id=1, replica_groups=mesh['ctx'=8,'tp'=4] {'ctx','tp'}, use_global_device_ids=true, to_apply=%region_1.0 | all-reduce | flops 1 | bytes 8 | tf_op jit(solution)/shard_map/pmax | solution.py:150
  111.4 1.2 copy_bitcast_fusion.1
  112.5 0.7 copy_dynamic-update-slice_fusion.1
  113.2 0.7 copy_dynamic-update-slice_fusion
  114.0 0.7 slice_bitcast_fusion.5
  114.7 5.9 %collective-permute-start.4 = (bf16[2,2,256,128]{3,1,2,0:T(2,128)(2,1)S(1)}, bf16[2,2,256,128]{3,1,2,0:T(2,128)(2,1)S(1)}, u32[]{:S(2)}, u32[]{:S(2)}) collective-permute-start(bf16[2,2,256,128]{3,1,2,0:T(2,128)(2,1)S(1)} %get-tuple-element.15), channel_id=1, source_target_pairs={{4,0},{8,4},{12,8},{16,12},{20,16},{24,20},{28,24},{5,1},{9,5},{13... | collective-permute-start | bytes 786440 | tf_op jit(solution)/shard_map/ppermute | solution.py:22
  120.6 1.3 collective-permute-start.7
  121.9 1.3 collective-permute-start.6
  123.2 1.9 %collective-permute-start.5 = (bf16[2,2,256,128]{3,1,2,0:T(2,128)(2,1)S(1)}, bf16[2,2,256,128]{3,1,2,0:T(2,128)(2,1)S(1)}, u32[]{:S(2)}, u32[]{:S(2)}) collective-permute-start(bf16[2,2,256,128]{3,1,2,0:T(2,128)(2,1)S(1)} %get-tuple-element.18), channel_id=1, source_target_pairs={{8,0},{12,4},{16,8},{20,12},{24,16},{28,20},{9,1},{13,5},{17,9},{2... | collective-permute-start | bytes 786440 | tf_op jit(solution)/shard_map/ppermute | solution.py:22
  125.1 1.2 copy_bitcast_fusion
  126.3 2.2 %collective-permute-done.4 = bf16[2,2,256,128]{3,1,2,0:T(2,128)(2,1)S(1)} collective-permute-done((bf16[2,2,256,128]{3,1,2,0:T(2,128)(2,1)S(1)}, bf16[2,2,256,128]{3,1,2,0:T(2,128)(2,1)S(1)}, u32[]{:S(2)}, u32[]{:S(2)}) %collective-permute-start.4) | collective-permute-done | bytes 262176 | tf_op jit(solution)/shard_map/ppermute | solution.py:22
  128.5 5.5 %collective-permute-done.7 = bf16[2,2,256,128]{3,1,2,0:T(2,128)(2,1)S(1)} collective-permute-done((bf16[2,2,256,128]{3,1,2,0:T(2,128)(2,1)S(1)}, bf16[2,2,256,128]{3,1,2,0:T(2,128)(2,1)S(1)}, u32[]{:S(2)}, u32[]{:S(2)}) %collective-permute-start.7) | collective-permute-done | bytes 262176 | tf_op jit(solution)/shard_map/ppermute | solution.py:22
  134.0 6.0 %collective-permute-done.6 = bf16[2,2,256,128]{3,1,2,0:T(2,128)(2,1)S(1)} collective-permute-done((bf16[2,2,256,128]{3,1,2,0:T(2,128)(2,1)S(1)}, bf16[2,2,256,128]{3,1,2,0:T(2,128)(2,1)S(1)}, u32[]{:S(2)}, u32[]{:S(2)}) %collective-permute-start.6) | collective-permute-done | bytes 262176 | tf_op jit(solution)/shard_map/ppermute | solution.py:22
  139.9 13.9 %collective-permute-done.5 = bf16[2,2,256,128]{3,1,2,0:T(2,128)(2,1)S(1)} collective-permute-done((bf16[2,2,256,128]{3,1,2,0:T(2,128)(2,1)S(1)}, bf16[2,2,256,128]{3,1,2,0:T(2,128)(2,1)S(1)}, u32[]{:S(2)}, u32[]{:S(2)}) %collective-permute-start.5) | collective-permute-done | bytes 262176 | tf_op jit(solution)/shard_map/ppermute | solution.py:22
  153.8 0.7 fusion.4
  154.5 0.9 slice_bitcast_fusion.7
  (14 shorter events, 0.1 us)
Async XLA Ops:
  0.6 14.8 %copy-start = (bf16[256,16,128]{2,1,0:T(8,128)(2,1)S(1)}, bf16[256,16,128]{2,1,0:T(8,128)(2,1)}, u32[]{:S(2)}) copy-start(bf16[256,16,128]{2,1,0:T(8,128)(2,1)} %param.5) | copy-start | bytes 3145732
  0.6 14.8 %copy-start.2 = (bf16[256,16,128]{2,1,0:T(8,128)(2,1)S(1)}, bf16[256,16,128]{2,1,0:T(8,128)(2,1)}, u32[]{:S(2)}) copy-start(bf16[256,16,128]{2,1,0:T(8,128)(2,1)} %param.8) | copy-start | bytes 3145732
  1.8 31.0 %collective-permute-start.3 = (bf16[2,2,256,128]{3,2,1,0:T(8,128)(2,1)S(1)}, bf16[2,2,256,128]{3,2,1,0:T(8,128)(2,1)S(1)}, u32[]{:S(2)}, u32[]{:S(2)}) collective-permute-start(bf16[2,2,256,128]{3,2,1,0:T(8,128)(2,1)S(1)} %maximum_bitcast_fusion), channel_id=1, source_target_pairs={{0,16},{4,20},{8,24},{12,28},{1,17},{5,21},{9,25},{13,29},{2,18},{... | collective-permute-start | bytes 786440 | tf_op jit(solution)/shard_map/ppermute | solution.py:22
  6.4 26.4 %collective-permute-start.2 = (bf16[2,2,256,128]{3,2,1,0:T(8,128)(2,1)S(1)}, bf16[2,2,256,128]{3,2,1,0:T(8,128)(2,1)S(1)}, u32[]{:S(2)}, u32[]{:S(2)}) collective-permute-start(bf16[2,2,256,128]{3,2,1,0:T(8,128)(2,1)S(1)} %maximum_bitcast_fusion), channel_id=1, source_target_pairs={{0,12},{4,16},{8,20},{12,24},{16,28},{1,13},{5,17},{9,21},{13,25},... | collective-permute-start | bytes 786440 | tf_op jit(solution)/shard_map/ppermute | solution.py:22
  7.7 24.1 %collective-permute-start.1 = (bf16[2,2,256,128]{3,2,1,0:T(8,128)(2,1)S(1)}, bf16[2,2,256,128]{3,2,1,0:T(8,128)(2,1)}, u32[]{:S(2)}, u32[]{:S(2)}) collective-permute-start(bf16[2,2,256,128]{3,2,1,0:T(8,128)(2,1)S(1)} %maximum_bitcast_fusion), channel_id=1, source_target_pairs={{0,8},{4,12},{8,16},{12,20},{16,24},{20,28},{1,9},{5,13},{9,17},{1... | collective-permute-start | bytes 786440 | tf_op jit(solution)/shard_map/ppermute | solution.py:22
  11.1 19.7 %collective-permute-start = (bf16[2,2,256,128]{3,2,1,0:T(8,128)(2,1)S(1)}, bf16[2,2,256,128]{3,2,1,0:T(8,128)(2,1)}, u32[]{:S(2)}, u32[]{:S(2)}) collective-permute-start(bf16[2,2,256,128]{3,2,1,0:T(8,128)(2,1)S(1)} %maximum_bitcast_fusion), channel_id=1, source_target_pairs={{0,4},{4,8},{8,12},{12,16},{16,20},{20,24},{24,28},{1,5},{5,9},{9,... | collective-permute-start | bytes 786440 | tf_op jit(solution)/shard_map/ppermute | solution.py:22
  113.9 11.2 %copy-start.1 = (bf16[2,2048,128]{2,1,0:T(8,128)(2,1)S(1)}, bf16[2,2048,128]{2,1,0:T(8,128)(2,1)}, u32[]{:S(2)}) copy-start(bf16[2,2048,128]{2,1,0:T(8,128)(2,1)} %get-tuple-element.11) | copy-start | bytes 3145732
  114.7 13.8 %collective-permute-start.4 = (bf16[2,2,256,128]{3,1,2,0:T(2,128)(2,1)S(1)}, bf16[2,2,256,128]{3,1,2,0:T(2,128)(2,1)S(1)}, u32[]{:S(2)}, u32[]{:S(2)}) collective-permute-start(bf16[2,2,256,128]{3,1,2,0:T(2,128)(2,1)S(1)} %get-tuple-element.15), channel_id=1, source_target_pairs={{4,0},{8,4},{12,8},{16,12},{20,16},{24,20},{28,24},{5,1},{9,5},{13... | collective-permute-start | bytes 786440 | tf_op jit(solution)/shard_map/ppermute | solution.py:22
  120.6 13.4 %collective-permute-start.7 = (bf16[2,2,256,128]{3,1,2,0:T(2,128)(2,1)S(1)}, bf16[2,2,256,128]{3,1,2,0:T(2,128)(2,1)S(1)}, u32[]{:S(2)}, u32[]{:S(2)}) collective-permute-start(bf16[2,2,256,128]{3,1,2,0:T(2,128)(2,1)S(1)} %get-tuple-element.16), channel_id=1, source_target_pairs={{16,0},{20,4},{24,8},{28,12},{17,1},{21,5},{25,9},{29,13},{18,2},{... | collective-permute-start | bytes 786440 | tf_op jit(solution)/shard_map/ppermute | solution.py:22
  121.9 18.0 %collective-permute-start.6 = (bf16[2,2,256,128]{3,1,2,0:T(2,128)(2,1)S(1)}, bf16[2,2,256,128]{3,1,2,0:T(2,128)(2,1)S(1)}, u32[]{:S(2)}, u32[]{:S(2)}) collective-permute-start(bf16[2,2,256,128]{3,1,2,0:T(2,128)(2,1)S(1)} %get-tuple-element.17), channel_id=1, source_target_pairs={{12,0},{16,4},{20,8},{24,12},{28,16},{13,1},{17,5},{21,9},{25,13},... | collective-permute-start | bytes 786440 | tf_op jit(solution)/shard_map/ppermute | solution.py:22
  123.2 30.6 %collective-permute-start.5 = (bf16[2,2,256,128]{3,1,2,0:T(2,128)(2,1)S(1)}, bf16[2,2,256,128]{3,1,2,0:T(2,128)(2,1)S(1)}, u32[]{:S(2)}, u32[]{:S(2)}) collective-permute-start(bf16[2,2,256,128]{3,1,2,0:T(2,128)(2,1)S(1)} %get-tuple-element.18), channel_id=1, source_target_pairs={{8,0},{12,4},{16,8},{20,12},{24,16},{28,20},{9,1},{13,5},{17,9},{2... | collective-permute-start | bytes 786440 | tf_op jit(solution)/shard_map/ppermute | solution.py:22
where the time goes:
time: 156 us; the launch traced here: 155 us
  blocking collectives  49.1 us (31%)
  waiting for transfers between devices  40.9 us (26%)
  Pallas kernels  28.8 us (18%)
  starting transfers between devices  22.2 us (14%)
  local copies, waits for them, and re-layouts  11.8 us (8%)
  other arithmetic  1.77 us (1%)
    pmax x1, blocking collectives, shards(): top_logit = lax.pmax(top[0, 0], ('ctx', 'tp'))  49.1 us
    ppermute x8, waiting for transfers between devices, shift(): return lax.ppermute(block, 'ctx', route)  40.9 us
    pallas_call x1, Pallas kernels, shards(): pl.pallas_call(functools.partial(kernel, heads, tokens), out_shape=(jax.S...  28.8 us
    ppermute x8, starting transfers between devices, shift(): return lax.ppermute(block, 'ctx', route)  22.2 us
  transfers between devices with their start and end apart: 8, of which 5 were waited for; matrix products, arithmetic and copies ran while one was open for 4% of the time, Pallas kernels for 0%

commit v1 on v0

v1 whole, which is shorter than its diff:
```python
import functools
import math

import jax
import jax.numpy as jnp
from jax import lax
from jax.experimental import pallas as pl
from jax.experimental.pallas import tpu as pltpu
from jax.sharding import PartitionSpec as P

REACH = 4
ROWS = 256
NEGATIVE = -1e30
F32 = jnp.float32
BF16 = jnp.bfloat16
NT = (((1,), (1,)), ((), ()))


def chunk_step(
    c, peak, g, heads, tokens, q_ref, do_ref, lo_ref, kv_ref, kt_ref, vt_ref,
    o_ref, dq_ref, dk_ref, dv_ref, s_ref, dp_ref, w_ref, ds_ref,
):
    tiles, width = kv_ref.shape[1], kv_ref.shape[4]
    scale = 1.0 / math.sqrt(width)
    base2 = scale * math.log2(math.e)
    rows = pl.ds(pl.multiple_of(c * ROWS, ROWS), ROWS)
    q = q_ref[g, rows, :]
    do = do_ref[g, rows, :]
    low = lo_ref[:, rows]
    key_place = lax.broadcasted_iota(jnp.int32, (tokens, ROWS), 0)
    query_place = (lax.broadcasted_iota(jnp.int32, (1, ROWS), 1) + c * ROWS) // heads
    top = jnp.full((1, ROWS), NEGATIVE, F32)
    for j in range(tiles):
        keys = pl.ds(j * tokens, tokens)
        s = lax.dot_general(kv_ref[g, j, 0], q, NT, preferred_element_type=F32)
        allowed = key_place >= low + j * tokens
        if j == 0:
            allowed = allowed & (key_place <= query_place)
        s = jnp.where(allowed, s, NEGATIVE)
        s_ref[keys, :] = s
        top = jnp.maximum(top, jnp.max(s, axis=0, keepdims=True))
    total = jnp.zeros((1, ROWS), F32)
    dot = jnp.zeros((1, ROWS), F32)
    for j in range(tiles):
        keys = pl.ds(j * tokens, tokens)
        p = jnp.exp2((s_ref[keys, :] - top) * base2)
        dp = lax.dot_general(kv_ref[g, j, 1], do, NT, preferred_element_type=F32)
        s_ref[keys, :] = p
        dp_ref[keys, :] = dp
        total = total + jnp.sum(p, axis=0, keepdims=True)
        dot = dot + jnp.sum(p * dp, axis=0, keepdims=True)
    inverse = 1.0 / total
    dot = dot * inverse
    for j in range(tiles):
        keys = pl.ds(j * tokens, tokens)
        p = s_ref[keys, :] * inverse
        w_ref[keys, :] = p.astype(BF16)
        ds_ref[keys, :] = (p * (dp_ref[keys, :] - dot)).astype(BF16)
    w = w_ref[...]
    ds = ds_ref[...]
    o = jnp.dot(vt_ref[...], w, preferred_element_type=F32)
    dq = jnp.dot(kt_ref[...], ds, preferred_element_type=F32) * scale
    o_ref[g, rows, :] = o.T.astype(BF16)
    dq_ref[g, rows, :] = dq.T.astype(BF16)
    dv_ref[...] += jnp.dot(w, do, preferred_element_type=F32)
    dk_ref[...] += jnp.dot(ds, q, preferred_element_type=F32)
    return jnp.maximum(peak, top)


def kernel(
    heads, tokens, sizes, q_ref, do_ref, lo_ref, own_ref,
    o_ref, dq_ref, dkv_ref, top_ref,
    kv_ref, out_ref, back_ref, peak_ref, peer_ref, kt_ref, vt_ref, dk_ref, dv_ref,
    s_ref, dp_ref, w_ref, ds_ref, send_sem, recv_sem, peak_send, peak_recv,
):
    groups, rows, width = q_ref.shape
    ranks, lanes = sizes
    chunks = rows // ROWS
    scale = 1.0 / math.sqrt(width)
    me = lax.axis_index("ctx")
    lane = lax.axis_index("tp")
    odd = lax.rem(me, 2) == 1
    even = lax.rem(me, 2) == 0
    mate = me + 1 - 2 * lax.rem(me, 2)
    has_ahead = me + 2 < ranks

    def flip(index, bit):
        return index + bit - 2 * bit * lax.rem(index // bit, 2)

    peers = [("ctx", flip(me, 1 << b)) for b in range((ranks - 1).bit_length())]
    peers += [("tp", flip(lane, 1 << b)) for b in range((lanes - 1).bit_length())]
    barrier = pltpu.get_barrier_semaphore()

    def greet(axis, index):
        pl.semaphore_signal(barrier, inc=1, device_id={axis: index}, device_id_type=pl.DeviceIdType.MESH)

    for axis, index in peers:
        greet(axis, index)
    pl.when(has_ahead)(lambda: greet("ctx", me + 2))
    pl.when(me >= 2)(lambda: greet("ctx", me - 2))
    pl.semaphore_wait(barrier, len(peers) + has_ahead.astype(jnp.int32) + (me >= 2).astype(jnp.int32))

    def move(g, k, src, dst, target):
        return pltpu.make_async_remote_copy(
            src_ref=src, dst_ref=dst, send_sem=send_sem.at[g, k], recv_sem=recv_sem.at[g, k],
            device_id={"ctx": target}, device_id_type=pl.DeviceIdType.MESH,
        )

    def hops(g):
        kv = lambda j: kv_ref.at[g, j]
        out = lambda k: out_ref.at[g, k]
        back = lambda k: back_ref.at[g, k]
        return {
            "a": (0, [(has_ahead, own_ref.at[g])], kv(2), me + 2, me >= 2),
            "b": (1, [(has_ahead & (me >= 2), kv(2))], kv(4), me + 2, me >= 4),
            "y1": (2, [(even, own_ref.at[g]), (odd & (me >= 3), kv(2))], kv(1), mate, me >= 1),
            "y3e": (3, [(even & (me >= 2), kv(2))], kv(3), mate, odd & (me >= 3)),
            "y3o": (4, [(odd & (me >= 5), kv(4))], kv(3), mate, even & (me >= 4)),
            "d1": (5, [(me >= 1, out(0))], back(0), mate, even | (me >= 3)),
            "d3": (6, [(me >= 3, out(2))], back(2), mate, (even & (me >= 2)) | (me >= 5)),
            "d4": (7, [(me >= 4, out(3))], back(3), me - 2, has_ahead & (me >= 2)),
            "d2": (8, [(me >= 2, out(1))], back(1), me - 2, has_ahead),
        }

    def start(g, name):
        slot, sources, dst, target, _ = hops(g)[name]
        for cond, src in sources:
            pl.when(cond)(lambda src=src: move(g, slot, src, dst, target).start())

    def arrive(g, name):
        slot, sources, dst, target, cond = hops(g)[name]
        pl.when(cond)(lambda: move(g, slot, sources[0][1], dst, target).wait_recv())

    def sent(g, name):
        slot, sources, dst, target, _ = hops(g)[name]
        for cond, src in sources:
            pl.when(cond)(lambda src=src: move(g, slot, src, dst, target).wait_send())

    def add(k, cond, g, slot):
        keys = pl.ds(k * tokens, tokens)

        @pl.when(cond)
        def _():
            dk_ref[g, keys, :] += back_ref[g, slot, 0].astype(F32)
            dv_ref[g, keys, :] += back_ref[g, slot, 1].astype(F32)

    def pack(g, k):
        keys = pl.ds(k * tokens, tokens)
        out_ref[g, k - 1, 0] = dk_ref[g, keys, :].astype(BF16)
        out_ref[g, k - 1, 1] = dv_ref[g, keys, :].astype(BF16)

    def back_one(g):
        pack(g, 1)
        pack(g, 3)
        start(g, "d3")
        start(g, "d1")

    def back_two(g):
        arrive(g, "d3")
        add(4, odd & (me >= 5), g, 2)
        add(2, even & (me >= 2), g, 2)
        pack(g, 4)
        start(g, "d4")

    def back_three(g):
        arrive(g, "d1")
        add(2, odd & (me >= 3), g, 0)
        add(0, even, g, 0)
        arrive(g, "d4")
        add(2, has_ahead & (me >= 2), g, 3)
        pack(g, 2)
        start(g, "d2")

    def back_last(g):
        arrive(g, "d2")
        add(0, has_ahead, g, 1)
        keys = pl.ds(0, tokens)
        dkv_ref[g, 0] = (dk_ref[g, keys, :] * scale).astype(BF16)
        dkv_ref[g, 1] = dv_ref[g, keys, :].astype(BF16)

    for g in range(groups):
        start(g, "a")
    for g in range(groups):
        pl.when(even)(lambda g=g: move(g, 2, own_ref.at[g], kv_ref.at[g, 1], mate).start())
    for g in range(groups):
        kv_ref[g, 0] = own_ref[g]
        for j in range(1, REACH + 1):
            @pl.when(me < j)
            def _(g=g, j=j):
                kv_ref[g, j] = jnp.zeros_like(kv_ref[g, j])
    dk_ref[...] = jnp.zeros_like(dk_ref)
    dv_ref[...] = jnp.zeros_like(dv_ref)
    for g in range(groups):
        arrive(g, "a")
        start(g, "b")
        pl.when(odd & (me >= 3))(lambda g=g: move(g, 2, kv_ref.at[g, 2], kv_ref.at[g, 1], mate).start())
        start(g, "y3e")
    def ready(g):
        arrive(g, "b")
        start(g, "y3o")
    def begin(g):
        for name in ("y1", "y3e", "y3o"):
            arrive(g, name)
        for j in range(REACH + 1):
            keys = pl.ds(j * tokens, tokens)
            kt_ref[:, keys] = kv_ref[g, j, 0].T
            vt_ref[:, keys] = kv_ref[g, j, 1].T
    ready(0)
    peak = jnp.full((1, ROWS), NEGATIVE, F32)
    plan = {(0, 0): [lambda: begin(0)]}
    for g in range(1, groups):
        plan.setdefault((g - 1, 3), []).append(lambda g=g: ready(g))
        plan.setdefault((g, 0), []).append(lambda g=g: (back_one(g - 1), begin(g)))
        plan.setdefault((g, 2), []).append(lambda g=g: back_two(g - 1))
        plan.setdefault((g, 4), []).append(lambda g=g: back_three(g - 1))
        plan.setdefault((g, 6), []).append(lambda g=g: back_last(g - 1))

    def step(t, peak):
        for (g, c), works in plan.items():
            @pl.when(t == g * chunks + c)
            def _(works=works):
                for work in works:
                    work()
        g = t // chunks
        return chunk_step(
            t - g * chunks, peak, g=g, heads=heads, tokens=tokens, q_ref=q_ref, do_ref=do_ref,
            lo_ref=lo_ref, kv_ref=kv_ref, kt_ref=kt_ref, vt_ref=vt_ref,
            o_ref=o_ref, dq_ref=dq_ref, dk_ref=dk_ref.at[g], dv_ref=dv_ref.at[g], s_ref=s_ref,
            dp_ref=dp_ref, w_ref=w_ref, ds_ref=ds_ref,
        )

    peak = lax.fori_loop(0, groups * chunks, step, peak)
    last = groups - 1
    back_one(last)
    best = jnp.broadcast_to(jnp.max(peak, axis=1, keepdims=True) * scale, top_ref.shape)

    def swap(r):
        axis, index = peers[r]
        return pltpu.make_async_remote_copy(
            src_ref=peak_ref.at[r], dst_ref=peer_ref.at[r], send_sem=peak_send.at[r],
            recv_sem=peak_recv.at[r], device_id={axis: index}, device_id_type=pl.DeviceIdType.MESH,
        )

    after = {1: back_two, 3: back_three}
    for r in range(len(peers)):
        peak_ref[r] = best
        swap(r).start()
        if r in after:
            after[r](last)
        swap(r).wait_recv()
        best = jnp.maximum(best, peer_ref[r])
    top_ref[...] = best
    back_last(last)
    for r in range(len(peers)):
        swap(r).wait_send()
    for g in range(groups):
        for name in ("a", "b", "y1", "y3e", "y3o", "d1", "d3", "d4", "d2"):
            sent(g, name)


def shards(sizes, query_rows, key_rows, value_rows, grad_rows, doc_ids):
    tokens, head_count, width = query_rows.shape
    groups = key_rows.shape[1]
    heads = head_count // groups
    me = lax.axis_index("ctx")
    own_ids = lax.dynamic_slice_in_dim(doc_ids, me * tokens, tokens, 0)
    first = jnp.sum((doc_ids[None, :] < own_ids[:, None]).astype(jnp.int32), axis=1)
    low = jnp.repeat(first - me * tokens, heads)[None, :]

    def by_group(x):
        return x.reshape(tokens, groups, heads, width).transpose(1, 0, 2, 3).reshape(groups, tokens * heads, width)

    def by_token(x):
        return x.reshape(groups, tokens, heads, width).transpose(1, 0, 2, 3).reshape(tokens, head_count, width)

    own = jnp.stack([key_rows, value_rows]).transpose(2, 0, 1, 3)
    tiles = REACH + 1
    keys = tiles * tokens
    rounds = sum((size - 1).bit_length() for size in sizes)
    vmem = pl.BlockSpec(memory_space=pltpu.VMEM)
    attended, query_grad, dkv, top = pl.pallas_call(
        functools.partial(kernel, heads, tokens, sizes),
        out_shape=(
            jax.ShapeDtypeStruct((groups, tokens * heads, width), BF16),
            jax.ShapeDtypeStruct((groups, tokens * heads, width), BF16),
            jax.ShapeDtypeStruct((groups, 2, tokens, width), BF16),
            jax.ShapeDtypeStruct((8, 128), F32),
        ),
        in_specs=[vmem] * 4,
        out_specs=(vmem,) * 4,
        scratch_shapes=[
            pltpu.VMEM((groups, tiles, 2, tokens, width), BF16),
            pltpu.VMEM((groups, REACH, 2, tokens, width), BF16),
            pltpu.VMEM((groups, REACH, 2, tokens, width), BF16),
            pltpu.VMEM((rounds, 8, 128), F32),
            pltpu.VMEM((rounds, 8, 128), F32),
            pltpu.VMEM((width, keys), BF16),
            pltpu.VMEM((width, keys), BF16),
            pltpu.VMEM((groups, keys, width), F32),
            pltpu.VMEM((groups, keys, width), F32),
            pltpu.VMEM((keys, ROWS), F32),
            pltpu.VMEM((keys, ROWS), F32),
            pltpu.VMEM((keys, ROWS), BF16),
            pltpu.VMEM((keys, ROWS), BF16),
            pltpu.SemaphoreType.DMA((groups, 9)),
            pltpu.SemaphoreType.DMA((groups, 9)),
            pltpu.SemaphoreType.DMA((rounds,)),
            pltpu.SemaphoreType.DMA((rounds,)),
        ],
        compiler_params=pltpu.CompilerParams(
            vmem_limit_bytes=50 << 20, collective_id=0, has_side_effects=True
        ),
    )(by_group(query_rows), by_group(grad_rows), low, own)
    result = dkv.transpose(1, 2, 0, 3)
    return by_token(attended), by_token(query_grad), result[0], result[1], top[0, 0]


def solution(mesh):
    part = P("ctx", "tp", None)
    return jax.shard_map(
        functools.partial(shards, (mesh.shape["ctx"], mesh.shape["tp"])),
        mesh=mesh,
        in_specs=(part, part, part, part, P()),
        out_specs=(part, part, part, part, P()),
        check_vma=False,
    )
```

time: 156 us -> 76.5 us (0.49)
  the two profiles are of different devices: /device:TPU:8 before, /device:TPU:0 now
where the time goes in v1:
time: 76.5 us; the launch traced here: 76.2 us
  Pallas kernels  66.5 us (87%)
  local copies, waits for them, and re-layouts  7.88 us (10%)
  other arithmetic  1.08 us (1%)
    pallas_call x1, Pallas kernels, shards(): pl.pallas_call(functools.partial(kernel, heads, tokens, sizes), out_shape...  66.5 us
    reshape x2, local copies, waits for them, and re-layouts, by_token(): x.reshape(groups, tokens, heads, width).transpose(1, 0, 2, 3)  2.3 us
    unnamed x6, local copies, waits for them, and re-layouts  1.59 us

profile of v1, /device:TPU:0, one launch (start us, length us, event | category | flops | bytes accessed | tf_op | source)
XLA Modules:
  0.0 76.2 jit_solution(17926869840555321399)
XLA Ops:
  0.6 0.0 copy-start
  0.6 0.0 copy-start.1
  0.7 0.9 %dynamic_slice.3 = s32[256]{0:T(256)S(1)} dynamic-slice(s32[2048]{0:T(1024)} %param.9, s32[]{:T(128)S(6)} %select_n.3), dynamic_slice_sizes={256} | dynamic-slice | bytes 2052 | tf_op jit(solution)/shard_map/dynamic_slice | solution.py:266
  1.6 1.0 %convert_reduce_fusion = s32[256]{0:T(256)S(1)} fusion(s32[2048]{0:T(1024)} %param.9, s32[256]{0:T(256)S(1)} %dynamic_slice.3), kind=kLoop, calls=%fused_computation | loop fusion | flops 1572608 | bytes 10240 | tf_op jit(solution)/shard_map/reduce_sum | solution.py:267
  2.6 0.1 broadcast_in_dim.2
  2.7 0.1 broadcast_in_dim_reshape.3.lo_ref
  2.8 1.0 %copy_bitcast_fusion.4 = (bf16[1,256,2,128]{3,1,0,2:T(8,128)(2,1)S(1)}, bf16[1,256,2,128]{3,1,0,2:T(8,128)(2,1)S(1)}) fusion(bf16[256,2,128]{2,1,0:T(2,128)(2,1)} %param.7, bf16[256,2,128]{2,1,0:T(2,128)(2,1)} %param.6), kind=kLoop, calls=%fused_computation.8 | loop fusion | bytes 524288 | tf_op jit(solution)/shard_map/stack | solution.py:276
  3.9 0.0 copy-done
  3.9 0.0 copy-done.1
  3.9 1.3 %copy_bitcast_fusion.2 = (bf16[2,2048,128]{2,1,0:T(8,128)(2,1)}, bf16[2,2048,128]{2,1,0:T(8,128)(2,1)S(1)}) fusion(bf16[256,16,128]{2,1,0:T(8,128)(2,1)S(1)} %copy-done, bf16[256,16,128]{2,1,0:T(8,128)(2,1)S(1)} %copy-done.1), kind=kLoop, calls=%fused_computation.3 | loop fusion | bytes 4194304 | tf_op jit(solution)/shard_map/reshape | solution.py:271
  5.2 66.5 %shard_map.92 = (bf16[2,2048,128]{2,1,0:T(8,128)(2,1)S(1)}, bf16[2,2048,128]{2,1,0:T(8,128)(2,1)S(1)}, bf16[2,2,256,128]{3,2,1,0:T(8,128)(2,1)S(1)}, f32[8,128]{1,0:T(8,128)S(1)}) custom-call(bf16[2,2048,128]{2,1,0:T(8,128)(2,1)S(1)} %get-tuple-element.33.q_ref, bf16[2,2048,128]{2,1,0:T(8,128)(2,1)} %get-tuple-element.32.do_ref, ...), custom_call_target="tpu_custom_call" | custom-call | tf_op jit(solution)/shard_map/pallas_call | solution.py:281
  71.8 0.5 slice.11
  72.3 1.1 %copy_bitcast_fusion.1 = bf16[256,16,128]{2,1,0:T(8,128)(2,1)} fusion(bf16[2,2048,128]{2,1,0:T(8,128)(2,1)S(1)} %get-tuple-element.9), kind=kLoop, calls=%fused_computation.2 | loop fusion | bytes 2097152 | tf_op jit(solution)/shard_map/reshape | solution.py:274
  73.5 0.8 %copy.33 = bf16[256,2,128]{2,1,0:T(2,128)(2,1)} copy(bf16[256,2,128]{2,0,1:T(8,128)(2,1)S(1)} %get-tuple-element.28) | data formatting | bytes 262144
  74.3 0.8 %copy.32 = bf16[256,2,128]{2,1,0:T(2,128)(2,1)} copy(bf16[256,2,128]{2,0,1:T(8,128)(2,1)S(1)} %get-tuple-element.29) | data formatting | bytes 262144
  75.1 1.1 %copy_bitcast_fusion = bf16[256,16,128]{2,1,0:T(8,128)(2,1)} fusion(bf16[2,2048,128]{2,1,0:T(8,128)(2,1)S(1)} %get-tuple-element.10), kind=kLoop, calls=%fused_computation.1 | loop fusion | bytes 2097152 | tf_op jit(solution)/shard_map/reshape | solution.py:274
  (3 shorter events, 0.1 us)
Async XLA Ops:
  0.6 3.3 %copy-start = (bf16[256,16,128]{2,1,0:T(8,128)(2,1)S(1)}, bf16[256,16,128]{2,1,0:T(8,128)(2,1)}, u32[]{:S(2)}) copy-start(bf16[256,16,128]{2,1,0:T(8,128)(2,1)} %param.5) | copy-start | bytes 3145732
  0.6 3.3 %copy-start.1 = (bf16[256,16,128]{2,1,0:T(8,128)(2,1)S(1)}, bf16[256,16,128]{2,1,0:T(8,128)(2,1)}, u32[]{:S(2)}) copy-start(bf16[256,16,128]{2,1,0:T(8,128)(2,1)} %param.8) | copy-start | bytes 3145732

commit v2 on v1

--- a/solution.py
+++ b/solution.py
@@ -10,68 +10,73 @@
 
 REACH = 4
 ROWS = 256
+FILL = 512
 NEGATIVE = -1e30
 F32 = jnp.float32
 BF16 = jnp.bfloat16
 NT = (((1,), (1,)), ((), ()))
 
 
+def fill(g, j, heads, tokens, q_ref, do_ref, lo_ref, kv_ref, kt_ref, vt_ref, s_ref, dp_ref, max_ref):
+    keys = pl.ds(j * tokens, tokens)
+    kt_ref[:, keys] = kv_ref[g, j, 0].T
+    vt_ref[:, keys] = kv_ref[g, j, 1].T
+    key_place = lax.broadcasted_iota(jnp.int32, (tokens, FILL), 0)
+
+    def body(c, carry):
+        rows = pl.ds(pl.multiple_of(c * FILL, FILL), FILL)
+        s = lax.dot_general(kv_ref[g, j, 0], q_ref[g, rows, :], NT, preferred_element_type=F32)
+        allowed = key_place >= lo_ref[:, rows] + j * tokens
+        if j == 0:
+            query_place = (lax.broadcasted_iota(jnp.int32, (1, FILL), 1) + c * FILL) // heads
+            allowed = allowed & (key_place <= query_place)
+        s = jnp.where(allowed, s, NEGATIVE)
+        s_ref[keys, rows] = s
+        top = jnp.max(s, axis=0, keepdims=True)
+        max_ref[:, rows] = top if j == 0 else jnp.maximum(max_ref[:, rows], top)
+        dp_ref[keys, rows] = lax.dot_general(
+            kv_ref[g, j, 1], do_ref[g, rows, :], NT, preferred_element_type=F32
+        )
+        return carry
+
+    lax.fori_loop(0, q_ref.shape[1] // FILL, body, 0)
+
+
 def chunk_step(
-    c, peak, g, heads, tokens, q_ref, do_ref, lo_ref, kv_ref, kt_ref, vt_ref,
-    o_ref, dq_ref, dk_ref, dv_ref, s_ref, dp_ref, w_ref, ds_ref,
+    c, g, tokens, o_ref, dq_ref, kt_ref, vt_ref, s_ref, dp_ref, w_ref, ds_ref, max_ref
 ):
-    tiles, width = kv_ref.shape[1], kv_ref.shape[4]
+    width = kt_ref.shape[0]
+    tiles = kt_ref.shape[1] // tokens
     scale = 1.0 / math.sqrt(width)
     base2 = scale * math.log2(math.e)
     rows = pl.ds(pl.multiple_of(c * ROWS, ROWS), ROWS)
-    q = q_ref[g, rows, :]
-    do = do_ref[g, rows, :]
-    low = lo_ref[:, rows]
-    key_place = lax.broadcasted_iota(jnp.int32, (tokens, ROWS), 0)
-    query_place = (lax.broadcasted_iota(jnp.int32, (1, ROWS), 1) + c * ROWS) // heads
-    top = jnp.full((1, ROWS), NEGATIVE, F32)
-    for j in range(tiles):
-        keys = pl.ds(j * tokens, tokens)
-        s = lax.dot_general(kv_ref[g, j, 0], q, NT, preferred_element_type=F32)
-        allowed = key_place >= low + j * tokens
-        if j == 0:
-            allowed = allowed & (key_place <= query_place)
-        s = jnp.where(allowed, s, NEGATIVE)
-        s_ref[keys, :] = s
-        top = jnp.maximum(top, jnp.max(s, axis=0, keepdims=True))
+    top = max_ref[:, rows]
     total = jnp.zeros((1, ROWS), F32)
     dot = jnp.zeros((1, ROWS), F32)
     for j in range(tiles):
         keys = pl.ds(j * tokens, tokens)
-        p = jnp.exp2((s_ref[keys, :] - top) * base2)
-        dp = lax.dot_general(kv_ref[g, j, 1], do, NT, preferred_element_type=F32)
-        s_ref[keys, :] = p
-        dp_ref[keys, :] = dp
+        p = jnp.exp2((s_ref[keys, rows] - top) * base2)
+        s_ref[keys, rows] = p
         total = total + jnp.sum(p, axis=0, keepdims=True)
-        dot = dot + jnp.sum(p * dp, axis=0, keepdims=True)
+        dot = dot + jnp.sum(p * dp_ref[keys, rows], axis=0, keepdims=True)
     inverse = 1.0 / total
     dot = dot * inverse
     for j in range(tiles):
         keys = pl.ds(j * tokens, tokens)
-        p = s_ref[keys, :] * inverse
-        w_ref[keys, :] = p.astype(BF16)
-        ds_ref[keys, :] = (p * (dp_ref[keys, :] - dot)).astype(BF16)
-    w = w_ref[...]
-    ds = ds_ref[...]
-    o = jnp.dot(vt_ref[...], w, preferred_element_type=F32)
-    dq = jnp.dot(kt_ref[...], ds, preferred_element_type=F32) * scale
+        p = s_ref[keys, rows] * inverse
+        w_ref[keys, rows] = p.astype(BF16)
+        ds_ref[keys, rows] = (p * (dp_ref[keys, rows] - dot)).astype(BF16)
+    o = jnp.dot(vt_ref[...], w_ref[:, rows], preferred_element_type=F32)
+    dq = jnp.dot(kt_ref[...], ds_ref[:, rows], preferred_element_type=F32) * scale
     o_ref[g, rows, :] = o.T.astype(BF16)
     dq_ref[g, rows, :] = dq.T.astype(BF16)
-    dv_ref[...] += jnp.dot(w, do, preferred_element_type=F32)
-    dk_ref[...] += jnp.dot(ds, q, preferred_element_type=F32)
-    return jnp.maximum(peak, top)
 
 
 def kernel(
     heads, tokens, sizes, q_ref, do_ref, lo_ref, own_ref,
     o_ref, dq_ref, dkv_ref, top_ref,
     kv_ref, out_ref, back_ref, peak_ref, peer_ref, kt_ref, vt_ref, dk_ref, dv_ref,
-    s_ref, dp_ref, w_ref, ds_ref, send_sem, recv_sem, peak_send, peak_recv,
+    s_ref, dp_ref, w_ref, ds_ref, max_ref, best_ref, send_sem, recv_sem, peak_send, peak_recv,
 ):
     groups, rows, width = q_ref.shape
     ranks, lanes = sizes
@@ -149,107 +154,144 @@
         out_ref[g, k - 1, 0] = dk_ref[g, keys, :].astype(BF16)
         out_ref[g, k - 1, 1] = dv_ref[g, keys, :].astype(BF16)
 
-    def back_one(g):
-        pack(g, 1)
-        pack(g, 3)
-        start(g, "d3")
-        start(g, "d1")
+    def finish(g, j):
+        keys = pl.ds(j * tokens, tokens)
+        dv_ref[g, keys, :] = jnp.dot(w_ref[keys, :], do_ref[g], preferred_element_type=F32)
+        dk_ref[g, keys, :] = jnp.dot(ds_ref[keys, :], q_ref[g], preferred_element_type=F32)
 
     def back_two(g):
         arrive(g, "d3")
         add(4, odd & (me >= 5), g, 2)
-        add(2, even & (me >= 2), g, 2)
         pack(g, 4)
         start(g, "d4")
 
     def back_three(g):
         arrive(g, "d1")
+        add(2, even & (me >= 2), g, 2)
         add(2, odd & (me >= 3), g, 0)
-        add(0, even, g, 0)
         arrive(g, "d4")
         add(2, has_ahead & (me >= 2), g, 3)
         pack(g, 2)
         start(g, "d2")
 
     def back_last(g):
+        add(0, even, g, 0)
         arrive(g, "d2")
         add(0, has_ahead, g, 1)
         keys = pl.ds(0, tokens)
         dkv_ref[g, 0] = (dk_ref[g, keys, :] * scale).astype(BF16)
         dkv_ref[g, 1] = dv_ref[g, keys, :].astype(BF16)
 
-    for g in range(groups):
+    def begin(g):
         start(g, "a")
-    for g in range(groups):
-        pl.when(even)(lambda g=g: move(g, 2, own_ref.at[g], kv_ref.at[g, 1], mate).start())
+        pl.when(even)(lambda: move(g, 2, own_ref.at[g], kv_ref.at[g, 1], mate).start())
+
+    def relay(g):
+        arrive(g, "a")
+        start(g, "b")
+        pl.when(odd & (me >= 3))(lambda: move(g, 2, kv_ref.at[g, 2], kv_ref.at[g, 1], mate).start())
+        start(g, "y3e")
+
+    def relay_last(g):
+        arrive(g, "b")
+        start(g, "y3o")
+
+    def swap(r):
+        axis, index = peers[r]
+        return pltpu.make_async_remote_copy(
+            src_ref=peak_ref.at[r], dst_ref=peer_ref.at[r], send_sem=peak_send.at[r],
+            recv_sem=peak_recv.at[r], device_id={axis: index}, device_id_type=pl.DeviceIdType.MESH,
+        )
+
+    def collect(r):
+        if r > 0:
+            swap(r - 1).wait_recv()
+            best_ref[...] = jnp.maximum(best_ref[...], peer_ref[r - 1])
+        if r < len(peers):
+            peak_ref[r] = best_ref[...]
+            swap(r).start()
+
+    def fill_tile(g, j):
+        fill(g, j, heads, tokens, q_ref, do_ref, lo_ref, kv_ref, kt_ref, vt_ref, s_ref, dp_ref, max_ref)
+
+    def note_peak():
+        best = jnp.max(max_ref[...], axis=1, keepdims=True) * scale
+        best_ref[...] = jnp.maximum(best_ref[...], jnp.broadcast_to(best, best_ref.shape))
+
+    def main(g, plan):
+        def step(c, carry):
+            for at, works in plan.items():
+                @pl.when(c == at)
+                def _(works=works):
+                    for work in works:
+                        work()
+            chunk_step(c, g, tokens, o_ref, dq_ref, kt_ref, vt_ref, s_ref, dp_ref, w_ref, ds_ref, max_ref)
+            return carry
+
+        lax.fori_loop(0, chunks, step, 0)
+
+    begin(0)
+    best_ref[...] = jnp.full_like(best_ref, NEGATIVE)
     for g in range(groups):
         kv_ref[g, 0] = own_ref[g]
         for j in range(1, REACH + 1):
             @pl.when(me < j)
             def _(g=g, j=j):
                 kv_ref[g, j] = jnp.zeros_like(kv_ref[g, j])
-    dk_ref[...] = jnp.zeros_like(dk_ref)
-    dv_ref[...] = jnp.zeros_like(dv_ref)
+    last = groups - 1
     for g in range(groups):
-        arrive(g, "a")
-        start(g, "b")
-        pl.when(odd & (me >= 3))(lambda g=g: move(g, 2, kv_ref.at[g, 2], kv_ref.at[g, 1], mate).start())
-        start(g, "y3e")
-    def ready(g):
-        arrive(g, "b")
-        start(g, "y3o")
-    def begin(g):
-        for name in ("y1", "y3e", "y3o"):
-            arrive(g, name)
-        for j in range(REACH + 1):
-            keys = pl.ds(j * tokens, tokens)
-            kt_ref[:, keys] = kv_ref[g, j, 0].T
-            vt_ref[:, keys] = kv_ref[g, j, 1].T
-    ready(0)
-    peak = jnp.full((1, ROWS), NEGATIVE, F32)
-    plan = {(0, 0): [lambda: begin(0)]}
-    for g in range(1, groups):
-        plan.setdefault((g - 1, 3), []).append(lambda g=g: ready(g))
-        plan.setdefault((g, 0), []).append(lambda g=g: (back_one(g - 1), begin(g)))
-        plan.setdefault((g, 2), []).append(lambda g=g: back_two(g - 1))
-        plan.setdefault((g, 4), []).append(lambda g=g: back_three(g - 1))
-        plan.setdefault((g, 6), []).append(lambda g=g: back_last(g - 1))
-
-    def step(t, peak):
-        for (g, c), works in plan.items():
-            @pl.when(t == g * chunks + c)
-            def _(works=works):
-                for work in works:
-                    work()
-        g = t // chunks
-        return chunk_step(
-            t - g * chunks, peak, g=g, heads=heads, tokens=tokens, q_ref=q_ref, do_ref=do_ref,
-            lo_ref=lo_ref, kv_ref=kv_ref, kt_ref=kt_ref, vt_ref=vt_ref,
-            o_ref=o_ref, dq_ref=dq_ref, dk_ref=dk_ref.at[g], dv_ref=dv_ref.at[g], s_ref=s_ref,
-            dp_ref=dp_ref, w_ref=w_ref, ds_ref=ds_ref,
-        )
-
-    peak = lax.fori_loop(0, groups * chunks, step, peak)
-    last = groups - 1
-    back_one(last)
-    best = jnp.broadcast_to(jnp.max(peak, axis=1, keepdims=True) * scale, top_ref.shape)
-
-    def swap(r):
-        axis, index = peers[r]
-        return pltpu.make_async_remote_copy(
-            src_ref=peak_ref.at[r], dst_ref=peer_ref.at[r], send_sem=peak_send.at[r],
-            recv_sem=peak_recv.at[r], device_id={axis: index}, device_id_type=pl.DeviceIdType.MESH,
-        )
-
-    after = {1: back_two, 3: back_three}
-    for r in range(len(peers)):
-        peak_ref[r] = best
-        swap(r).start()
-        if r in after:
-            after[r](last)
-        swap(r).wait_recv()
-        best = jnp.maximum(best, peer_ref[r])
-    top_ref[...] = best
+        fill_tile(g, 0)
+        if g == 0:
+            relay(0)
+            fill_tile(0, 2)
+            arrive(0, "y1")
+            fill_tile(0, 1)
+            relay_last(0)
+            if last > 0:
+                begin(1)
+            fill_tile(0, 4)
+            arrive(0, "y3e")
+            arrive(0, "y3o")
+            fill_tile(0, 3)
+        else:
+            fill_tile(g, 2)
+            arrive(g, "y1")
+            fill_tile(g, 1)
+            back_two(g - 1)
+            fill_tile(g, 4)
+            arrive(g, "y3e")
+            arrive(g, "y3o")
+            fill_tile(g, 3)
+        note_peak()
+        plan = {}
+        if g > 0:
+            plan.setdefault(1, []).append(lambda g=g: back_three(g - 1))
+            plan.setdefault(4, []).append(lambda g=g: back_last(g - 1))
+        if g < last:
+            plan.setdefault(2, []).append(lambda g=g: relay(g + 1))
+            plan.setdefault(5, []).append(lambda g=g: relay_last(g + 1))
+            if g + 1 < last:
+                plan.setdefault(6, []).append(lambda g=g: begin(g + 2))
+        else:
+            for r in range(min(len(peers) + 1, chunks)):
+                plan.setdefault(r, []).append(lambda r=r: collect(r))
+        main(g, plan)
+        finish(g, 3)
+        pack(g, 3)
+        start(g, "d3")
+        finish(g, 1)
+        pack(g, 1)
+        start(g, "d1")
+        finish(g, 4)
+        if g == last:
+            back_two(g)
+        finish(g, 2)
+        if g == last:
+            back_three(g)
+        finish(g, 0)
+    for r in range(chunks, len(peers) + 1):
+        collect(r)
+    top_ref[...] = best_ref[...]
     back_last(last)
     for r in range(len(peers)):
         swap(r).wait_send()
@@ -298,10 +340,12 @@
             pltpu.VMEM((width, keys), BF16),
             pltpu.VMEM((groups, keys, width), F32),
             pltpu.VMEM((groups, keys, width), F32),
-            pltpu.VMEM((keys, ROWS), F32),
-            pltpu.VMEM((keys, ROWS), F32),
-            pltpu.VMEM((keys, ROWS), BF16),
-            pltpu.VMEM((keys, ROWS), BF16),
+            pltpu.VMEM((keys, tokens * heads), F32),
+            pltpu.VMEM((keys, tokens * heads), F32),
+            pltpu.VMEM((keys, tokens * heads), BF16),
+            pltpu.VMEM((keys, tokens * heads), BF16),
+            pltpu.VMEM((1, tokens * heads), F32),
+            pltpu.VMEM((8, 128), F32),
             pltpu.SemaphoreType.DMA((groups, 9)),
             pltpu.SemaphoreType.DMA((groups, 9)),
             pltpu.SemaphoreType.DMA((rounds,)),

time: 76.5 us -> 76 us (level)
  no operation moved by 1% of the time
where the time goes in v2:
time: 76 us; the launch traced here: 75.8 us
  Pallas kernels  66.1 us (87%)
  local copies, waits for them, and re-layouts  7.88 us (10%)
  other arithmetic  1.08 us (1%)
    pallas_call x1, Pallas kernels, shards(): pl.pallas_call(functools.partial(kernel, heads, tokens, sizes), out_shape...  66.1 us
    reshape x2, local copies, waits for them, and re-layouts, by_token(): x.reshape(groups, tokens, heads, width).transpose(1, 0, 2, 3)  2.3 us
    unnamed x6, local copies, waits for them, and re-layouts  1.59 us

profile of v2, /device:TPU:0, one launch (start us, length us, event | category | flops | bytes accessed | tf_op | source)
XLA Modules:
  0.0 75.8 jit_solution(856035263181286136)
XLA Ops:
  0.6 0.0 copy-start
  0.6 0.0 copy-start.1
  0.7 0.9 %dynamic_slice.3 = s32[256]{0:T(256)S(1)} dynamic-slice(s32[2048]{0:T(1024)} %param.9, s32[]{:T(128)S(6)} %select_n.3), dynamic_slice_sizes={256} | dynamic-slice | bytes 2052 | tf_op jit(solution)/shard_map/dynamic_slice | solution.py:308
  1.6 1.0 %convert_reduce_fusion = s32[256]{0:T(256)S(1)} fusion(s32[2048]{0:T(1024)} %param.9, s32[256]{0:T(256)S(1)} %dynamic_slice.3), kind=kLoop, calls=%fused_computation | loop fusion | flops 1572608 | bytes 10240 | tf_op jit(solution)/shard_map/reduce_sum | solution.py:309
  2.6 0.1 broadcast_in_dim.2
  2.7 0.1 broadcast_in_dim_reshape.3.lo_ref
  2.8 1.0 %copy_bitcast_fusion.4 = (bf16[1,256,2,128]{3,1,0,2:T(8,128)(2,1)S(1)}, bf16[1,256,2,128]{3,1,0,2:T(8,128)(2,1)S(1)}) fusion(bf16[256,2,128]{2,1,0:T(2,128)(2,1)} %param.7, bf16[256,2,128]{2,1,0:T(2,128)(2,1)} %param.6), kind=kLoop, calls=%fused_computation.8 | loop fusion | bytes 524288 | tf_op jit(solution)/shard_map/stack | solution.py:318
  3.9 0.0 copy-done
  3.9 0.0 copy-done.1
  3.9 1.3 %copy_bitcast_fusion.2 = (bf16[2,2048,128]{2,1,0:T(8,128)(2,1)}, bf16[2,2048,128]{2,1,0:T(8,128)(2,1)S(1)}) fusion(bf16[256,16,128]{2,1,0:T(8,128)(2,1)S(1)} %copy-done, bf16[256,16,128]{2,1,0:T(8,128)(2,1)S(1)} %copy-done.1), kind=kLoop, calls=%fused_computation.3 | loop fusion | bytes 4194304 | tf_op jit(solution)/shard_map/reshape | solution.py:313
  5.2 66.1 %shard_map.92 = (bf16[2,2048,128]{2,1,0:T(8,128)(2,1)S(1)}, bf16[2,2048,128]{2,1,0:T(8,128)(2,1)S(1)}, bf16[2,2,256,128]{3,2,1,0:T(8,128)(2,1)S(1)}, f32[8,128]{1,0:T(8,128)S(1)}) custom-call(bf16[2,2048,128]{2,1,0:T(8,128)(2,1)S(1)} %get-tuple-element.33.q_ref, bf16[2,2048,128]{2,1,0:T(8,128)(2,1)} %get-tuple-element.32.do_ref, ...), custom_call_target="tpu_custom_call" | custom-call | tf_op jit(solution)/shard_map/pallas_call | solution.py:323
  71.4 0.5 slice.11
  71.9 1.1 %copy_bitcast_fusion.1 = bf16[256,16,128]{2,1,0:T(8,128)(2,1)} fusion(bf16[2,2048,128]{2,1,0:T(8,128)(2,1)S(1)} %get-tuple-element.9), kind=kLoop, calls=%fused_computation.2 | loop fusion | bytes 2097152 | tf_op jit(solution)/shard_map/reshape | solution.py:316
  73.0 0.8 %copy.33 = bf16[256,2,128]{2,1,0:T(2,128)(2,1)} copy(bf16[256,2,128]{2,0,1:T(8,128)(2,1)S(1)} %get-tuple-element.28) | data formatting | bytes 262144
  73.8 0.8 %copy.32 = bf16[256,2,128]{2,1,0:T(2,128)(2,1)} copy(bf16[256,2,128]{2,0,1:T(8,128)(2,1)S(1)} %get-tuple-element.29) | data formatting | bytes 262144
  74.6 1.1 %copy_bitcast_fusion = bf16[256,16,128]{2,1,0:T(8,128)(2,1)} fusion(bf16[2,2048,128]{2,1,0:T(8,128)(2,1)S(1)} %get-tuple-element.10), kind=kLoop, calls=%fused_computation.1 | loop fusion | bytes 2097152 | tf_op jit(solution)/shard_map/reshape | solution.py:316
  (3 shorter events, 0.1 us)
Async XLA Ops:
  0.6 3.3 %copy-start = (bf16[256,16,128]{2,1,0:T(8,128)(2,1)S(1)}, bf16[256,16,128]{2,1,0:T(8,128)(2,1)}, u32[]{:S(2)}) copy-start(bf16[256,16,128]{2,1,0:T(8,128)(2,1)} %param.5) | copy-start | bytes 3145732
  0.6 3.3 %copy-start.1 = (bf16[256,16,128]{2,1,0:T(8,128)(2,1)S(1)}, bf16[256,16,128]{2,1,0:T(8,128)(2,1)}, u32[]{:S(2)}) copy-start(bf16[256,16,128]{2,1,0:T(8,128)(2,1)} %param.8) | copy-start | bytes 3145732

commit v3 on v2

--- a/solution.py
+++ b/solution.py
@@ -10,7 +10,7 @@
 
 REACH = 4
 ROWS = 256
-FILL = 512
+FILL = 256
 NEGATIVE = -1e30
 F32 = jnp.float32
 BF16 = jnp.bfloat16
@@ -281,14 +281,14 @@
         start(g, "d3")
         finish(g, 1)
         pack(g, 1)
-        start(g, "d1")
         finish(g, 4)
+        finish(g, 2)
         if g == last:
             back_two(g)
-        finish(g, 2)
+        start(g, "d1")
+        finish(g, 0)
         if g == last:
             back_three(g)
-        finish(g, 0)
     for r in range(chunks, len(peers) + 1):
         collect(r)
     top_ref[...] = best_ref[...]

time: 76 us -> 79.1 us (1.041)
  Pallas kernels: 66.1 us -> 68.9 us
    pallas_call x1, Pallas kernels: 66.1 us -> 68.9 us  [shards(): pl.pallas_call(functools.partial(kernel, heads, tokens, sizes), out_shape...]
where the time goes in v3:
time: 79.1 us; the launch traced here: 78.6 us
  Pallas kernels  68.9 us (87%)
  local copies, waits for them, and re-layouts  7.88 us (10%)
  other arithmetic  1.08 us (1%)
    pallas_call x1, Pallas kernels, shards(): pl.pallas_call(functools.partial(kernel, heads, tokens, sizes), out_shape...  68.9 us
    reshape x2, local copies, waits for them, and re-layouts, by_token(): x.reshape(groups, tokens, heads, width).transpose(1, 0, 2, 3)  2.3 us
    unnamed x6, local copies, waits for them, and re-layouts  1.59 us

profile of v3, /device:TPU:0, one launch (start us, length us, event | category | flops | bytes accessed | tf_op | source)
XLA Modules:
  0.0 78.6 jit_solution(6420542314109148956)
XLA Ops:
  0.6 0.0 copy-start
  0.6 0.0 copy-start.1
  0.7 0.9 %dynamic_slice.3 = s32[256]{0:T(256)S(1)} dynamic-slice(s32[2048]{0:T(1024)} %param.9, s32[]{:T(128)S(6)} %select_n.3), dynamic_slice_sizes={256} | dynamic-slice | bytes 2052 | tf_op jit(solution)/shard_map/dynamic_slice | solution.py:308
  1.6 1.0 %convert_reduce_fusion = s32[256]{0:T(256)S(1)} fusion(s32[2048]{0:T(1024)} %param.9, s32[256]{0:T(256)S(1)} %dynamic_slice.3), kind=kLoop, calls=%fused_computation | loop fusion | flops 1572608 | bytes 10240 | tf_op jit(solution)/shard_map/reduce_sum | solution.py:309
  2.6 0.1 broadcast_in_dim.2
  2.7 0.1 broadcast_in_dim_reshape.3.lo_ref
  2.8 1.0 %copy_bitcast_fusion.4 = (bf16[1,256,2,128]{3,1,0,2:T(8,128)(2,1)S(1)}, bf16[1,256,2,128]{3,1,0,2:T(8,128)(2,1)S(1)}) fusion(bf16[256,2,128]{2,1,0:T(2,128)(2,1)} %param.7, bf16[256,2,128]{2,1,0:T(2,128)(2,1)} %param.6), kind=kLoop, calls=%fused_computation.8 | loop fusion | bytes 524288 | tf_op jit(solution)/shard_map/stack | solution.py:318
  3.9 0.0 copy-done
  3.9 0.0 copy-done.1
  3.9 1.3 %copy_bitcast_fusion.2 = (bf16[2,2048,128]{2,1,0:T(8,128)(2,1)}, bf16[2,2048,128]{2,1,0:T(8,128)(2,1)S(1)}) fusion(bf16[256,16,128]{2,1,0:T(8,128)(2,1)S(1)} %copy-done, bf16[256,16,128]{2,1,0:T(8,128)(2,1)S(1)} %copy-done.1), kind=kLoop, calls=%fused_computation.3 | loop fusion | bytes 4194304 | tf_op jit(solution)/shard_map/reshape | solution.py:313
  5.2 68.9 %shard_map.92 = (bf16[2,2048,128]{2,1,0:T(8,128)(2,1)S(1)}, bf16[2,2048,128]{2,1,0:T(8,128)(2,1)S(1)}, bf16[2,2,256,128]{3,2,1,0:T(8,128)(2,1)S(1)}, f32[8,128]{1,0:T(8,128)S(1)}) custom-call(bf16[2,2048,128]{2,1,0:T(8,128)(2,1)S(1)} %get-tuple-element.33.q_ref, bf16[2,2048,128]{2,1,0:T(8,128)(2,1)} %get-tuple-element.32.do_ref, ...), custom_call_target="tpu_custom_call" | custom-call | tf_op jit(solution)/shard_map/pallas_call | solution.py:323
  74.2 0.5 slice.11
  74.7 1.1 %copy_bitcast_fusion.1 = bf16[256,16,128]{2,1,0:T(8,128)(2,1)} fusion(bf16[2,2048,128]{2,1,0:T(8,128)(2,1)S(1)} %get-tuple-element.9), kind=kLoop, calls=%fused_computation.2 | loop fusion | bytes 2097152 | tf_op jit(solution)/shard_map/reshape | solution.py:316
  75.9 0.8 %copy.33 = bf16[256,2,128]{2,1,0:T(2,128)(2,1)} copy(bf16[256,2,128]{2,0,1:T(8,128)(2,1)S(1)} %get-tuple-element.28) | data formatting | bytes 262144
  76.7 0.8 %copy.32 = bf16[256,2,128]{2,1,0:T(2,128)(2,1)} copy(bf16[256,2,128]{2,0,1:T(8,128)(2,1)S(1)} %get-tuple-element.29) | data formatting | bytes 262144
  77.4 1.1 %copy_bitcast_fusion = bf16[256,16,128]{2,1,0:T(8,128)(2,1)} fusion(bf16[2,2048,128]{2,1,0:T(8,128)(2,1)S(1)} %get-tuple-element.10), kind=kLoop, calls=%fused_computation.1 | loop fusion | bytes 2097152 | tf_op jit(solution)/shard_map/reshape | solution.py:316
  (3 shorter events, 0.1 us)
Async XLA Ops:
  0.6 3.3 %copy-start = (bf16[256,16,128]{2,1,0:T(8,128)(2,1)S(1)}, bf16[256,16,128]{2,1,0:T(8,128)(2,1)}, u32[]{:S(2)}) copy-start(bf16[256,16,128]{2,1,0:T(8,128)(2,1)} %param.5) | copy-start | bytes 3145732
  0.6 3.3 %copy-start.1 = (bf16[256,16,128]{2,1,0:T(8,128)(2,1)S(1)}, bf16[256,16,128]{2,1,0:T(8,128)(2,1)}, u32[]{:S(2)}) copy-start(bf16[256,16,128]{2,1,0:T(8,128)(2,1)} %param.8) | copy-start | bytes 3145732
